TPU v7x, 256 devices: a whole 4x4x8 slice. The times are simulated.
256 devices in a mesh: dp: 8 (over x, z_lo), ctx: 32 (over y, z_hi, core).
Axes of the slice: x: 4, y: 4, z: 8 (z_hi: 4, z_lo: 2; z = z_hi * 2 + z_lo), core: 2. Of those that a mesh axis runs over, the one named last changes fastest.
Arguments:
- query_gate: bfloat16 [8, 4096, 2048], P('dp', 'ctx'), may hold values from -6 to 6
- key_gate: bfloat16 [8, 4096, 2048], P('dp', 'ctx'), may hold values from -6 to 6
- value_in: bfloat16 [8, 4096, 2048], P('dp', 'ctx'), may hold values from -6 to 6
- out_grad: bfloat16 [8, 4096, 2048], P('dp', 'ctx'), may hold values from -6 to 6
- filter_taps: float32 [2048, 4096], P('ctx'), may hold values from -2 to 2
Outputs:
- mixed_out: bfloat16 [8, 4096, 2048], P('dp', 'ctx')
- query_grad: bfloat16 [8, 4096, 2048], P('dp', 'ctx')
- key_grad: bfloat16 [8, 4096, 2048], P('dp', 'ctx')
- value_grad: bfloat16 [8, 4096, 2048], P('dp', 'ctx')
- filter_grad: float32 [2048, 4096], P('ctx', 'dp')
All inputs are finite; a program needn't handle non-finite values.
Results may differ from a plain program's by a relative error of at most 0.017.
Values may be sent and summed in bfloat16 or wider, within the bound.
A program may use at most 128 MiB of HBM per device.

v0:
```python
import functools
import math

import jax
import jax.numpy as jnp
import numpy as np
from jax import lax
from jax.experimental import pallas as pl
from jax.experimental.pallas import tpu as pltpu
from jax.sharding import PartitionSpec as P

MESH = pl.DeviceIdType.MESH
LANES = 128
HALF = 32
BINS = 33
GROUP = 16
CHUNK = 11
ROOT = math.sqrt(0.5)


def tables():
    step = np.arange(LANES, dtype=np.float64)
    angle = 2.0 * np.pi * ((step[:, None] * step[None, :]) % LANES) / LANES
    cos, sin = np.cos(angle), np.sin(angle)
    forward = np.block([[cos, -sin], [sin, cos]])
    inverse = np.block([[cos, sin], [-sin, cos]]) / (64.0 * LANES)
    turn = 2.0 * np.pi * (np.arange(BINS, dtype=np.float64)[:, None] * step[None, :]) / (64.0 * LANES)
    twist = np.concatenate([np.cos(turn), np.sin(turn)], axis=1)
    return (
        jnp.asarray(forward, jnp.bfloat16),
        jnp.asarray(inverse, jnp.bfloat16),
        jnp.asarray(twist, jnp.float32),
    )


def add(a, b):
    return (a[0] + b[0], a[1] + b[1])


def sub(a, b):
    return (a[0] - b[0], a[1] - b[1])


def turned(a, part):
    part = part % 1.0
    if part == 0.0:
        return a
    if part == 0.25:
        return (-a[1], a[0])
    if part == 0.5:
        return (-a[0], -a[1])
    if part == 0.75:
        return (a[1], -a[0])
    cos, sin = math.cos(2.0 * math.pi * part), math.sin(2.0 * math.pi * part)
    if part in (0.125, 0.375, 0.625, 0.875):
        c, s = math.copysign(1.0, cos), math.copysign(1.0, sin)
        real = a[0] - a[1] if c == s else a[0] + a[1]
        imag = a[0] + a[1] if c == s else a[1] - a[0]
        return ((c * ROOT) * real, (c * ROOT) * imag)
    return (a[0] * cos - a[1] * sin, a[0] * sin + a[1] * cos)


def four(x, sign):
    a, b = add(x[0], x[2]), sub(x[0], x[2])
    c, d = add(x[1], x[3]), sub(x[1], x[3])
    e = turned(d, 0.25 * sign)
    return [add(a, c), add(b, e), sub(a, c), sub(b, e)]


def eight(x, sign):
    even, odd = four(x[0::2], sign), four(x[1::2], sign)
    odd = [turned(odd[k], sign * k / 8.0) for k in range(4)]
    return [add(even[k], odd[k]) for k in range(4)] + [sub(even[k], odd[k]) for k in range(4)]


def real_eight(x):
    a, b = x[0] + x[4], x[0] - x[4]
    c, d = x[2] + x[6], x[2] - x[6]
    e, f = x[1] + x[5], x[1] - x[5]
    g, h = x[3] + x[7], x[3] - x[7]
    p, q = ROOT * (f - h), ROOT * (f + h)
    return [
        (a + c) + (e + g),
        (b + p, -d - q),
        (a - c, g - e),
        (b - p, d - q),
        (a + c) - (e + g),
    ]


def block_forward(x):
    cols = [[] for _ in range(5)]
    for b in range(8):
        x0, x1, x2, x3 = x[b], x[8 + b], x[16 + b], x[24 + b]
        p, q = x0 + x2, x1 + x3
        m, n = ROOT * (x1 - x3), ROOT * q
        cols[0].append(p + q)
        cols[1].append(turned((x0 + m, -x2 - n), -b / 64.0))
        cols[2].append(turned((x0 - x2, x3 - x1), -2 * b / 64.0))
        cols[3].append(turned((x0 - m, x2 - n), -3 * b / 64.0))
        cols[4].append(p - q)
    out = [None] * BINS
    for d, value in enumerate(real_eight(cols[0])):
        out[8 * d] = value
    for c in (1, 2, 3):
        for d, value in enumerate(eight(cols[c], -1)):
            k = c + 8 * d
            if k <= 32:
                out[k] = value
            else:
                out[64 - k] = (value[0], -value[1])
    r = cols[4]
    u = four([turned((r[b], -r[b + 4]), -b / 16.0) for b in range(4)], -1)
    out[4], out[20] = u[0], u[1]
    out[28] = (u[2][0], -u[2][1])
    out[12] = (u[3][0], -u[3][1])
    return out


def real_back(t0, t1, t2, t3, t4, count):
    a, b = t0 + t4, t0 - t4
    r2, i2 = 2.0 * t2[0], 2.0 * t2[1]
    even = [a + r2, b - i2, a - r2, b + i2]
    odd = [
        2.0 * (t1[0] + t3[0]),
        (2.0 * ROOT) * ((t1[0] - t1[1]) - (t3[0] + t3[1])),
        2.0 * (t3[1] - t1[1]),
        (2.0 * ROOT) * ((t3[0] - t3[1]) - (t1[0] + t1[1])),
    ]
    first = [even[k] + odd[k] for k in range(4)]
    if count == 4:
        return first
    return first + [even[k] - odd[k] for k in range(4)]


def block_inverse(v):
    t = [None] * 5
    t[0] = real_back(v[0], v[8], v[16], v[24], v[32], 8)
    for c in (1, 2, 3):
        u = []
        for d in range(8):
            k = c + 8 * d
            u.append(v[k] if k <= 32 else (v[64 - k][0], -v[64 - k][1]))
        u = eight(u, 1)
        t[c] = [turned(u[b], b * c / 64.0) for b in range(8)]
    g = four([v[4], v[20], (v[28][0], -v[28][1]), (v[12][0], -v[12][1])], 1)
    g = [turned(g[b], b / 16.0) for b in range(4)]
    t[4] = [2.0 * g[b][0] for b in range(4)] + [-2.0 * g[b][1] for b in range(4)]
    out = [None] * HALF
    for b in range(8):
        for a, value in enumerate(real_back(t[0][b], t[1][b], t[2][b], t[3][b], t[4][b], 4)):
            out[8 * a + b] = value
    return out


def analyse(read, twist, packed, channels):
    def body(g, carry):
        rows = pl.ds(pl.multiple_of(g * GROUP, GROUP), GROUP)
        bins = block_forward([read(j, rows) for j in range(HALF)])
        for k in range(BINS):
            if k == 0:
                real, imag = bins[0], jnp.zeros_like(bins[0])
            else:
                cos, sin = twist[k : k + 1, :LANES], twist[k : k + 1, LANES:]
                if k == 32:
                    real, imag = bins[k] * cos, -(bins[k] * sin)
                else:
                    real = bins[k][0] * cos + bins[k][1] * sin
                    imag = bins[k][1] * cos - bins[k][0] * sin
            packed[k, rows, :LANES] = real.astype(jnp.bfloat16)
            packed[k, rows, LANES:] = imag.astype(jnp.bfloat16)
        return carry

    lax.fori_loop(0, channels // GROUP, body, 0)


def synthesise(wide, twist, write, channels):
    def body(g, carry):
        rows = pl.ds(pl.multiple_of(g * GROUP, GROUP), GROUP)
        bins = []
        for k in range(BINS):
            real, imag = wide[k, rows, :LANES], wide[k, rows, LANES:]
            cos, sin = twist[k : k + 1, :LANES], twist[k : k + 1, LANES:]
            if k == 0:
                bins.append(real)
            elif k == 32:
                bins.append(real * cos - imag * sin)
            else:
                bins.append((real * cos - imag * sin, real * sin + imag * cos))
        for j, value in enumerate(block_inverse(bins)):
            write(j, rows, value)
        return carry

    lax.fori_loop(0, channels // GROUP, body, 0)


def chunks(body):
    def step(i, carry):
        body(pl.ds(i * CHUNK, CHUNK))
        return carry

    lax.fori_loop(0, BINS // CHUNK, step, 0)


def times(rows, matrix):
    flat = rows.reshape(-1, 2 * LANES)
    out = jnp.dot(flat, matrix, preferred_element_type=jnp.float32)
    return out.reshape(rows.shape)


def times_conj(a, b):
    ar, ai, br, bi = a[..., :LANES], a[..., LANES:], b[..., :LANES], b[..., LANES:]
    return jnp.concatenate([ar * br + ai * bi, ar * bi - ai * br], axis=-1)


def times_plain(a, b):
    ar, ai, br, bi = a[..., :LANES], a[..., LANES:], b[..., :LANES], b[..., LANES:]
    return jnp.concatenate([ar * br - ai * bi, ar * bi + ai * br], axis=-1)


def mixing(
    peers,
    query,
    key,
    value,
    grad,
    taps_in,
    forward_in,
    inverse_in,
    twist_in,
    conv_out,
    back_out,
    filter_out,
    gate,
    taps,
    forward,
    inverse,
    twist,
    sent,
    got,
    replied,
    answer,
    packed,
    wide,
    filter_spec,
    mixed_spec,
    grad_spec,
    term,
    term_got,
    half,
    half_got,
    load_sem,
    send_sem,
    recv_sem,
    term_sem,
    half_sem,
    store_sem,
):
    me = lax.axis_index("ctx")
    dp = lax.axis_index("dp")
    line, side = dp // 2, dp % 2
    channels = taps.shape[0]
    chunk_rows = sent.shape[2]

    barrier = pltpu.get_barrier_semaphore()

    def greet(i, carry):
        pl.semaphore_signal(
            barrier, inc=1, device_id={"ctx": lax.rem(me + i, peers)}, device_id_type=MESH
        )
        return carry

    lax.fori_loop(1, peers, greet, 0)
    for i in range(1, 4):
        pl.semaphore_signal(
            barrier, inc=1, device_id={"dp": lax.rem(line + i, 4) * 2 + side}, device_id_type=MESH
        )
    pl.semaphore_signal(barrier, inc=1, device_id={"dp": line * 2 + 1 - side}, device_id_type=MESH)

    loads = [
        pltpu.make_async_copy(source, target, load_sem.at[n])
        for n, (source, target) in enumerate(
            [
                (key, gate.at[0]),
                (value, gate.at[1]),
                (query, gate.at[2]),
                (grad, gate.at[3]),
                (taps_in, taps),
                (forward_in, forward),
                (inverse_in, inverse),
                (twist_in, twist),
            ]
        )
    ]
    for load in loads:
        load.start()

    def gated(first, second, slot):
        def body(t, carry):
            lanes = pl.ds(pl.multiple_of(t * LANES, LANES), LANES)
            product = gate[first, :, lanes].astype(jnp.float32) * gate[second, :, lanes].astype(jnp.float32)
            flipped = jnp.transpose(product).astype(jnp.bfloat16)
            sent[slot, pl.ds(2 * t, 2)] = flipped.reshape(2, LANES // 2, LANES)
            return carry

        lax.fori_loop(0, peers // 2, body, 0)
        got[slot, me] = sent[slot, me]

    def scatter(source, target, slot, sem_base):
        def body(i, carry):
            peer = lax.rem(me + i, peers)
            pltpu.make_async_remote_copy(
                src_ref=source.at[slot, peer],
                dst_ref=target.at[slot, me],
                send_sem=send_sem.at[sem_base + slot],
                recv_sem=recv_sem.at[sem_base + slot],
                device_id={"ctx": peer},
                device_id_type=MESH,
            ).start()
            return carry

        lax.fori_loop(1, peers, body, 0)

    def whole(source, target, slot, sem_base):
        part = pl.ds(0, peers - 1)
        return pltpu.make_async_remote_copy(
            src_ref=source.at[slot, part],
            dst_ref=target.at[slot, part],
            send_sem=send_sem.at[sem_base + slot],
            recv_sem=recv_sem.at[sem_base + slot],
            device_id={"ctx": lax.rem(me + 1, peers)},
            device_id_type=MESH,
        )

    loads[0].wait()
    loads[1].wait()
    gated(0, 1, 0)
    pl.semaphore_wait(barrier, peers - 1 + 4)
    scatter(sent, got, 0, 0)
    loads[2].wait()
    loads[3].wait()
    gated(2, 3, 1)
    scatter(sent, got, 1, 0)
    for load in loads[4:]:
        load.wait()

    analyse(lambda j, rows: taps[rows, j * LANES : (j + 1) * LANES], twist, packed, channels)

    def filter_step(k):
        filter_spec[k] = times(packed[k], forward[...])

    chunks(filter_step)

    def convolve(slot, spectrum, product):
        whole(sent, got, slot, 0).wait_recv()
        analyse(lambda j, rows: got[slot, j, rows, :].astype(jnp.float32), twist, packed, channels)

        def step(k):
            spec = times(packed[k], forward[...])
            spectrum[k] = spec
            wide[k] = times(product(filter_spec[k], spec).astype(jnp.bfloat16), inverse[...])

        chunks(step)

        def write(j, rows, values):
            replied[slot, j, rows, :] = values.astype(jnp.bfloat16)

        synthesise(wide, twist, write, channels)
        answer[slot, me] = replied[slot, me]
        scatter(replied, answer, slot, 2)

    convolve(0, mixed_spec, times_plain)
    convolve(1, grad_spec, times_conj)

    def term_step(k):
        wide[k] = times(times_conj(mixed_spec[k], grad_spec[k]).astype(jnp.bfloat16), inverse[...])

    chunks(term_step)

    def write_term(j, rows, values):
        term[j, rows, :] = values.astype(jnp.bfloat16)

    synthesise(wide, twist, write_term, channels)

    hops = []
    for i in range(1, 4):
        other = lax.rem(line + i, 4)
        hops.append(
            pltpu.make_async_remote_copy(
                src_ref=term.at[pl.ds(other * 8, 8)],
                dst_ref=term_got.at[i - 1],
                send_sem=term_sem.at[i - 1],
                recv_sem=term_sem.at[i + 2],
                device_id={"dp": other * 2 + side},
                device_id_type=MESH,
            )
        )
    for hop in hops:
        hop.start()
    for hop in hops:
        hop.wait_recv()

    def total(which):
        mine = term[pl.ds(line * 8 + which * 4, 4)].astype(jnp.float32)
        for i in range(3):
            mine += term_got[i, pl.ds(which * 4, 4)].astype(jnp.float32)
        return mine

    half[...] = total(1 - side).astype(jnp.bfloat16)
    cross = pltpu.make_async_remote_copy(
        src_ref=half,
        dst_ref=half_got,
        send_sem=half_sem.at[0],
        recv_sem=half_sem.at[1],
        device_id={"dp": line * 2 + 1 - side},
        device_id_type=MESH,
    )
    cross.start()
    kept = total(side)
    cross.wait_recv()
    kept += half_got[...].astype(jnp.float32)
    for j in range(4):
        filter_out[:, j * LANES : (j + 1) * LANES] = kept[j]

    whole(replied, answer, 0, 2).wait_recv()
    conv_store = pltpu.make_async_copy(answer.at[0], conv_out, store_sem.at[0])
    conv_store.start()
    whole(replied, answer, 1, 2).wait_recv()
    back_store = pltpu.make_async_copy(answer.at[1], back_out, store_sem.at[1])
    back_store.start()
    for slot in range(2):
        whole(sent, got, slot, 0).wait_send()
        whole(replied, answer, slot, 2).wait_send()
    for hop in hops:
        hop.wait_send()
    cross.wait_send()
    conv_store.wait()
    back_store.wait()


def finish(scale, query, key, value, grad, conv, back, total, mixed_out, query_grad, key_grad, value_grad, filter_grad):
    def tokens(ref):
        rows = ref[...].reshape(-1, LANES).astype(jnp.float32)
        return jnp.transpose(rows)

    conv_wide = tokens(conv)
    mixed_out[0] = (query[0].astype(jnp.float32) * conv_wide).astype(jnp.bfloat16)
    query_grad[0] = (grad[0].astype(jnp.float32) * conv_wide).astype(jnp.bfloat16)
    back_wide = tokens(back)
    key_grad[0] = (back_wide * value[0].astype(jnp.float32)).astype(jnp.bfloat16)
    value_grad[0] = (back_wide * key[0].astype(jnp.float32)).astype(jnp.bfloat16)
    filter_grad[...] = total[...] * scale


def shards(query_gate, key_gate, value_in, out_grad, filter_taps):
    _, block, width = query_gate.shape
    channels, seq_len = filter_taps.shape
    peers = lax.axis_size("ctx")
    parts = lax.axis_size("dp")
    forward, inverse, twist = tables()
    anywhere = pl.BlockSpec(memory_space=pl.ANY)
    in_vmem = pl.BlockSpec(memory_space=pltpu.VMEM)
    planes = (peers, channels, LANES)
    spectrum = pltpu.VMEM((BINS, channels, 2 * LANES), jnp.float32)
    share = seq_len // parts
    conv, back, total = pl.pallas_call(
        functools.partial(mixing, peers),
        out_shape=(
            jax.ShapeDtypeStruct(planes, jnp.bfloat16),
            jax.ShapeDtypeStruct(planes, jnp.bfloat16),
            jax.ShapeDtypeStruct((channels, share), jnp.float32),
        ),
        in_specs=[anywhere] * 8,
        out_specs=(anywhere, anywhere, in_vmem),
        scratch_shapes=[
            pltpu.VMEM((4, block, width), jnp.bfloat16),
            pltpu.VMEM((channels, seq_len), jnp.float32),
            pltpu.VMEM((2 * LANES, 2 * LANES), jnp.bfloat16),
            pltpu.VMEM((2 * LANES, 2 * LANES), jnp.bfloat16),
            pltpu.VMEM((BINS, 2 * LANES), jnp.float32),
            pltpu.VMEM((2,) + planes, jnp.bfloat16),
            pltpu.VMEM((2,) + planes, jnp.bfloat16),
            pltpu.VMEM((2,) + planes, jnp.bfloat16),
            pltpu.VMEM((2,) + planes, jnp.bfloat16),
            pltpu.VMEM((BINS, channels, 2 * LANES), jnp.bfloat16),
            spectrum,
            spectrum,
            spectrum,
            spectrum,
            pltpu.VMEM(planes, jnp.bfloat16),
            pltpu.VMEM((3, 8, channels, LANES), jnp.bfloat16),
            pltpu.VMEM((4, channels, LANES), jnp.bfloat16),
            pltpu.VMEM((4, channels, LANES), jnp.bfloat16),
            pltpu.SemaphoreType.DMA((8,)),
            pltpu.SemaphoreType.DMA((4,)),
            pltpu.SemaphoreType.DMA((4,)),
            pltpu.SemaphoreType.DMA((6,)),
            pltpu.SemaphoreType.DMA((2,)),
            pltpu.SemaphoreType.DMA((2,)),
        ],
        compiler_params=pltpu.CompilerParams(
            collective_id=0, has_side_effects=True, vmem_limit_bytes=48 << 20
        ),
        name="mixing",
    )(
        query_gate[0],
        key_gate[0],
        value_in[0],
        out_grad[0],
        filter_taps,
        forward,
        inverse,
        twist,
    )

    steps = 8
    wide = width // steps
    token_spec = pl.BlockSpec((1, block, wide), lambda t: (0, 0, t))
    plane_spec = pl.BlockSpec((peers // steps, channels, LANES), lambda t: (t, 0, 0))
    filter_block = pl.BlockSpec((channels // steps, share), lambda t: (t, 0))
    tokens = jax.ShapeDtypeStruct(query_gate.shape, jnp.bfloat16)
    return pl.pallas_call(
        functools.partial(finish, (seq_len * parts) ** (-0.5)),
        grid=(steps,),
        out_shape=(tokens,) * 4 + (jax.ShapeDtypeStruct((channels, share), jnp.float32),),
        in_specs=[token_spec] * 4 + [plane_spec] * 2 + [filter_block],
        out_specs=(token_spec,) * 4 + (filter_block,),
        name="finish",
    )(query_gate, key_gate, value_in, out_grad, conv, back, total)


def solution(mesh):
    placed = (
        P("dp", "ctx", None),
        P("dp", "ctx", None),
        P("dp", "ctx", None),
        P("dp", "ctx", None),
        P("ctx", None),
    )
    return jax.shard_map(
        shards,
        mesh=mesh,
        in_specs=placed,
        out_specs=(
            P("dp", "ctx", None),
            P("dp", "ctx", None),
            P("dp", "ctx", None),
            P("dp", "ctx", None),
            P("ctx", "dp"),
        ),
        check_vma=False,
    )
```

profile of v0, /device:TPU:1, one launch (start us, length us, event | category | flops | bytes accessed | tf_op | source)
XLA Modules:
  0.0 76.2 jit_solution(14284265634884121587)
XLA Ops:
  0.6 0.0 copy-start
  0.6 1.0 %copy-done = bf16[1,128,2048]{2,1,0:T(8,128)(2,1)S(1)} copy-done((bf16[1,128,2048]{2,1,0:T(8,128)(2,1)S(1)}, bf16[1,128,2048]{2,1,0:T(8,128)(2,1)}, u32[]{:S(2)}) %copy-start) | copy-done | bytes 524312
  1.7 0.0 copy-start.1
  1.7 1.0 %copy-done.1 = bf16[1,128,2048]{2,1,0:T(8,128)(2,1)S(1)} copy-done((bf16[1,128,2048]{2,1,0:T(8,128)(2,1)S(1)}, bf16[1,128,2048]{2,1,0:T(8,128)(2,1)}, u32[]{:S(2)}) %copy-start.1) | copy-done | bytes 524312
  2.7 0.0 copy-start.2
  2.7 1.0 %copy-done.2 = bf16[1,128,2048]{2,1,0:T(8,128)(2,1)S(1)} copy-done((bf16[1,128,2048]{2,1,0:T(8,128)(2,1)S(1)}, bf16[1,128,2048]{2,1,0:T(8,128)(2,1)}, u32[]{:S(2)}) %copy-start.2) | copy-done | bytes 524312
  3.8 0.0 copy-start.3
  3.8 1.0 %copy-done.3 = bf16[1,128,2048]{2,1,0:T(8,128)(2,1)S(1)} copy-done((bf16[1,128,2048]{2,1,0:T(8,128)(2,1)S(1)}, bf16[1,128,2048]{2,1,0:T(8,128)(2,1)}, u32[]{:S(2)}) %copy-start.3) | copy-done | bytes 524312
  4.8 0.0 copy-start.4
  4.8 1.2 %copy-done.4 = f32[64,4096]{1,0:T(8,128)S(1)} copy-done((f32[64,4096]{1,0:T(8,128)S(1)}, f32[64,4096]{1,0:T(8,128)}, u32[]{:S(2)}) %copy-start.4) | copy-done | bytes 1048600
  6.0 0.0 copy-start.8
  6.0 0.9 %copy-done.8 = bf16[256,256]{1,0:T(8,128)(2,1)S(1)} copy-done((bf16[256,256]{1,0:T(8,128)(2,1)S(1)}, bf16[256,256]{1,0:T(8,128)(2,1)}, u32[]{:S(2)}) %copy-start.8) | copy-done | bytes 131096
  6.9 0.0 copy-start.9
  6.9 0.9 %copy-done.9 = bf16[256,256]{1,0:T(8,128)(2,1)S(1)} copy-done((bf16[256,256]{1,0:T(8,128)(2,1)S(1)}, bf16[256,256]{1,0:T(8,128)(2,1)}, u32[]{:S(2)}) %copy-start.9) | copy-done | bytes 131096
  7.8 0.0 copy-start.10
  7.8 0.8 %copy-done.10 = f32[33,256]{1,0:T(8,128)S(1)} copy-done((f32[33,256]{1,0:T(8,128)S(1)}, f32[33,256]{1,0:T(8,128)}, u32[]{:S(2)}) %copy-start.10) | copy-done | bytes 33816
  8.6 59.2 %mixing.1 = (bf16[32,64,128]{2,1,0:T(8,128)(2,1)S(1)}, bf16[32,64,128]{2,1,0:T(8,128)(2,1)S(1)}, f32[64,512]{1,0:T(8,128)S(1)}) custom-call(bf16[128,2048]{1,0:T(8,128)(2,1)S(1)} %bitcast.4, bf16[128,2048]{1,0:T(8,128)(2,1)S(1)} %bitcast.5, bf16[128,2048]{1,0:T(8,128)(2,1)S(1)} %bitcast.6, bf16[128,2048]{1,0:T(8,128)(2,1)S(1)} %bitcast.7, ...), custom_call_target="tpu_custom_call" | custom-call | tf_op jit(solution)/shard_map/mixing/pallas_call | solution.py:466
  67.8 0.0 copy-start.5
  67.8 0.8 %copy-done.5 = bf16[32,64,128]{2,1,0:T(8,128)(2,1)} copy-done((bf16[32,64,128]{2,1,0:T(8,128)(2,1)}, bf16[32,64,128]{2,1,0:T(8,128)(2,1)S(1)}, u32[]{:S(2)}) %copy-start.5) | copy-done | bytes 524312
  68.6 0.0 copy-start.6
  68.6 0.8 %copy-done.6 = bf16[32,64,128]{2,1,0:T(8,128)(2,1)} copy-done((bf16[32,64,128]{2,1,0:T(8,128)(2,1)}, bf16[32,64,128]{2,1,0:T(8,128)(2,1)S(1)}, u32[]{:S(2)}) %copy-start.6) | copy-done | bytes 524312
  69.4 0.0 copy-start.7
  69.4 0.6 copy-done.7
  70.0 6.2 %finish.1 = (bf16[1,128,2048]{2,1,0:T(8,128)(2,1)}, bf16[1,128,2048]{2,1,0:T(8,128)(2,1)}, bf16[1,128,2048]{2,1,0:T(8,128)(2,1)}, bf16[1,128,2048]{2,1,0:T(8,128)(2,1)}, f32[64,512]{1,0:T(8,128)}) custom-call(bf16[1,128,2048]{2,1,0:T(8,128)(2,1)} %query.1, bf16[1,128,2048]{2,1,0:T(8,128)(2,1)} %key.1, bf16[1,128,2048]{2,1,0:T(8,128)(2,1)} %value.1, ...), custom_call_target="tpu_custom_call" | custom-call | tf_op jit(solution)/shard_map/finish/pallas_call | solution.py:522
Async XLA Ops:
  0.6 1.0 %copy-start = (bf16[1,128,2048]{2,1,0:T(8,128)(2,1)S(1)}, bf16[1,128,2048]{2,1,0:T(8,128)(2,1)}, u32[]{:S(2)}) copy-start(bf16[1,128,2048]{2,1,0:T(8,128)(2,1)} %query.1) | copy-start | bytes 1572868
  1.7 1.0 %copy-start.1 = (bf16[1,128,2048]{2,1,0:T(8,128)(2,1)S(1)}, bf16[1,128,2048]{2,1,0:T(8,128)(2,1)}, u32[]{:S(2)}) copy-start(bf16[1,128,2048]{2,1,0:T(8,128)(2,1)} %key.1) | copy-start | bytes 1572868
  2.7 1.0 %copy-start.2 = (bf16[1,128,2048]{2,1,0:T(8,128)(2,1)S(1)}, bf16[1,128,2048]{2,1,0:T(8,128)(2,1)}, u32[]{:S(2)}) copy-start(bf16[1,128,2048]{2,1,0:T(8,128)(2,1)} %value.1) | copy-start | bytes 1572868
  3.8 1.0 %copy-start.3 = (bf16[1,128,2048]{2,1,0:T(8,128)(2,1)S(1)}, bf16[1,128,2048]{2,1,0:T(8,128)(2,1)}, u32[]{:S(2)}) copy-start(bf16[1,128,2048]{2,1,0:T(8,128)(2,1)} %grad.1) | copy-start | bytes 1572868
  4.8 1.2 %copy-start.4 = (f32[64,4096]{1,0:T(8,128)S(1)}, f32[64,4096]{1,0:T(8,128)}, u32[]{:S(2)}) copy-start(f32[64,4096]{1,0:T(8,128)} %taps_in.1) | copy-start | bytes 3145732
  6.0 0.9 %copy-start.8 = (bf16[256,256]{1,0:T(8,128)(2,1)S(1)}, bf16[256,256]{1,0:T(8,128)(2,1)}, u32[]{:S(2)}) copy-start(bf16[256,256]{1,0:T(8,128)(2,1)} %constant.7.clone.inverse_in) | copy-start | bytes 393220
  6.9 0.9 %copy-start.9 = (bf16[256,256]{1,0:T(8,128)(2,1)S(1)}, bf16[256,256]{1,0:T(8,128)(2,1)}, u32[]{:S(2)}) copy-start(bf16[256,256]{1,0:T(8,128)(2,1)} %constant.6.clone.forward_in) | copy-start | bytes 393220
  7.8 0.8 %copy-start.10 = (f32[33,256]{1,0:T(8,128)S(1)}, f32[33,256]{1,0:T(8,128)}, u32[]{:S(2)}) copy-start(f32[33,256]{1,0:T(8,128)} %constant.8.clone.twist_in) | copy-start | bytes 101380
  67.8 0.8 %copy-start.5 = (bf16[32,64,128]{2,1,0:T(8,128)(2,1)}, bf16[32,64,128]{2,1,0:T(8,128)(2,1)S(1)}, u32[]{:S(2)}) copy-start(bf16[32,64,128]{2,1,0:T(8,128)(2,1)S(1)} %get-tuple-element.8.conv) | copy-start | bytes 1572868
  68.6 0.8 %copy-start.6 = (bf16[32,64,128]{2,1,0:T(8,128)(2,1)}, bf16[32,64,128]{2,1,0:T(8,128)(2,1)S(1)}, u32[]{:S(2)}) copy-start(bf16[32,64,128]{2,1,0:T(8,128)(2,1)S(1)} %get-tuple-element.9.back) | copy-start | bytes 1572868
  69.4 0.6 copy-start.7
where the time goes:
time: 77 us; the launch traced here: 76.2 us
  Pallas kernels  65.4 us (85%)
  local copies, waits for them, and re-layouts  10.2 us (13%)
    pallas_call x1, Pallas kernels, shards(): pl.pallas_call(functools.partial(mixing, peers), out_shape=(jax.ShapeDtyp...  59.2 us
    unnamed x22, local copies, waits for them, and re-layouts  10.2 us
    pallas_call x1, Pallas kernels, shards(): pl.pallas_call(functools.partial(finish, (seq_len * parts) ** (-0.5)), gr...  6.24 us

commit v1 on v0

--- a/solution.py
+++ b/solution.py
@@ -220,6 +220,7 @@
 
 def mixing(
     peers,
+    scale,
     query,
     key,
     value,
@@ -228,8 +229,10 @@
     forward_in,
     inverse_in,
     twist_in,
-    conv_out,
-    back_out,
+    mixed_out,
+    query_grad,
+    key_grad,
+    value_grad,
     filter_out,
     gate,
     taps,
@@ -254,13 +257,12 @@
     recv_sem,
     term_sem,
     half_sem,
-    store_sem,
+    back_sem,
 ):
     me = lax.axis_index("ctx")
     dp = lax.axis_index("dp")
     line, side = dp // 2, dp % 2
     channels = taps.shape[0]
-    chunk_rows = sent.shape[2]
 
     barrier = pltpu.get_barrier_semaphore()
 
@@ -309,11 +311,12 @@
     def scatter(source, target, slot, sem_base):
         def body(i, carry):
             peer = lax.rem(me + i, peers)
+            last = sem_base + slot == 3
             pltpu.make_async_remote_copy(
                 src_ref=source.at[slot, peer],
                 dst_ref=target.at[slot, me],
                 send_sem=send_sem.at[sem_base + slot],
-                recv_sem=recv_sem.at[sem_base + slot],
+                recv_sem=back_sem.at[me] if last else recv_sem.at[sem_base + slot],
                 device_id={"ctx": peer},
                 device_id_type=MESH,
             ).start()
@@ -420,36 +423,57 @@
     cross.wait_recv()
     kept += half_got[...].astype(jnp.float32)
     for j in range(4):
-        filter_out[:, j * LANES : (j + 1) * LANES] = kept[j]
+        filter_out[:, j * LANES : (j + 1) * LANES] = kept[j] * scale
+
+    def tile(slot, t, first, second, first_out, second_out):
+        lanes = pl.ds(pl.multiple_of(t * LANES, LANES), LANES)
+        rows = answer[slot, pl.ds(2 * t, 2)].reshape(LANES, LANES)
+        wide_rows = jnp.transpose(rows.astype(jnp.float32))
+        first_out[0, :, lanes] = (gate[first, :, lanes].astype(jnp.float32) * wide_rows).astype(jnp.bfloat16)
+        second_out[0, :, lanes] = (gate[second, :, lanes].astype(jnp.float32) * wide_rows).astype(jnp.bfloat16)
 
     whole(replied, answer, 0, 2).wait_recv()
-    conv_store = pltpu.make_async_copy(answer.at[0], conv_out, store_sem.at[0])
-    conv_store.start()
-    whole(replied, answer, 1, 2).wait_recv()
-    back_store = pltpu.make_async_copy(answer.at[1], back_out, store_sem.at[1])
-    back_store.start()
+
+    def conv_tile(t, carry):
+        tile(0, t, 2, 3, mixed_out, query_grad)
+        return carry
+
+    lax.fori_loop(0, peers // 2, conv_tile, 0)
+
+    def back_tile(i, carry):
+        t = lax.rem(me // 2 + peers // 2 - i, peers // 2)
+        for source in (2 * t, 2 * t + 1):
+
+            @pl.when(source != me)
+            def _():
+                pltpu.make_async_remote_copy(
+                    src_ref=replied.at[1, source],
+                    dst_ref=answer.at[1, source],
+                    send_sem=send_sem.at[3],
+                    recv_sem=back_sem.at[source],
+                    device_id={"ctx": lax.rem(me + 1, peers)},
+                    device_id_type=MESH,
+                ).wait_recv()
+
+        tile(1, t, 1, 0, key_grad, value_grad)
+        return carry
+
+    lax.fori_loop(0, peers // 2, back_tile, 0)
     for slot in range(2):
         whole(sent, got, slot, 0).wait_send()
         whole(replied, answer, slot, 2).wait_send()
     for hop in hops:
         hop.wait_send()
     cross.wait_send()
-    conv_store.wait()
-    back_store.wait()
-
-
-def finish(scale, query, key, value, grad, conv, back, total, mixed_out, query_grad, key_grad, value_grad, filter_grad):
-    def tokens(ref):
-        rows = ref[...].reshape(-1, LANES).astype(jnp.float32)
-        return jnp.transpose(rows)
-
-    conv_wide = tokens(conv)
-    mixed_out[0] = (query[0].astype(jnp.float32) * conv_wide).astype(jnp.bfloat16)
-    query_grad[0] = (grad[0].astype(jnp.float32) * conv_wide).astype(jnp.bfloat16)
-    back_wide = tokens(back)
-    key_grad[0] = (back_wide * value[0].astype(jnp.float32)).astype(jnp.bfloat16)
-    value_grad[0] = (back_wide * key[0].astype(jnp.float32)).astype(jnp.bfloat16)
-    filter_grad[...] = total[...] * scale
+
+
+def finish(*refs):
+    held, out, sem = refs[:5], refs[5:10], refs[10]
+    copies = [pltpu.make_async_copy(a, b, sem.at[n]) for n, (a, b) in enumerate(zip(held, out))]
+    for copy in copies:
+        copy.start()
+    for copy in copies:
+        copy.wait()
 
 
 def shards(query_gate, key_gate, value_in, out_grad, filter_taps):
@@ -458,20 +482,18 @@
     peers = lax.axis_size("ctx")
     parts = lax.axis_size("dp")
     forward, inverse, twist = tables()
-    anywhere = pl.BlockSpec(memory_space=pl.ANY)
+    in_hbm = pl.BlockSpec(memory_space=pltpu.HBM)
     in_vmem = pl.BlockSpec(memory_space=pltpu.VMEM)
     planes = (peers, channels, LANES)
     spectrum = pltpu.VMEM((BINS, channels, 2 * LANES), jnp.float32)
     share = seq_len // parts
-    conv, back, total = pl.pallas_call(
-        functools.partial(mixing, peers),
-        out_shape=(
-            jax.ShapeDtypeStruct(planes, jnp.bfloat16),
-            jax.ShapeDtypeStruct(planes, jnp.bfloat16),
-            jax.ShapeDtypeStruct((channels, share), jnp.float32),
-        ),
-        in_specs=[anywhere] * 8,
-        out_specs=(anywhere, anywhere, in_vmem),
+    tokens = jax.ShapeDtypeStruct(query_gate.shape, jnp.bfloat16)
+    shapes = (tokens,) * 4 + (jax.ShapeDtypeStruct((channels, share), jnp.float32),)
+    held = pl.pallas_call(
+        functools.partial(mixing, peers, (seq_len * parts) ** (-0.5)),
+        out_shape=tuple(pltpu.VMEM(a.shape, a.dtype) for a in shapes),
+        in_specs=[in_hbm] * 8,
+        out_specs=(in_vmem,) * 5,
         scratch_shapes=[
             pltpu.VMEM((4, block, width), jnp.bfloat16),
             pltpu.VMEM((channels, seq_len), jnp.float32),
@@ -496,37 +518,36 @@
             pltpu.SemaphoreType.DMA((4,)),
             pltpu.SemaphoreType.DMA((6,)),
             pltpu.SemaphoreType.DMA((2,)),
-            pltpu.SemaphoreType.DMA((2,)),
+            pltpu.SemaphoreType.DMA((peers,)),
         ],
         compiler_params=pltpu.CompilerParams(
-            collective_id=0, has_side_effects=True, vmem_limit_bytes=48 << 20
+            collective_id=0, has_side_effects=True, vmem_limit_bytes=32 << 20
         ),
         name="mixing",
     )(
-        query_gate[0],
-        key_gate[0],
-        value_in[0],
-        out_grad[0],
-        filter_taps,
-        forward,
-        inverse,
-        twist,
+        *(
+            pltpu.with_memory_space_constraint(a, pltpu.HBM)
+            for a in (
+                query_gate[0],
+                key_gate[0],
+                value_in[0],
+                out_grad[0],
+                filter_taps,
+                forward,
+                inverse,
+                twist,
+            )
+        )
     )
 
-    steps = 8
-    wide = width // steps
-    token_spec = pl.BlockSpec((1, block, wide), lambda t: (0, 0, t))
-    plane_spec = pl.BlockSpec((peers // steps, channels, LANES), lambda t: (t, 0, 0))
-    filter_block = pl.BlockSpec((channels // steps, share), lambda t: (t, 0))
-    tokens = jax.ShapeDtypeStruct(query_gate.shape, jnp.bfloat16)
     return pl.pallas_call(
-        functools.partial(finish, (seq_len * parts) ** (-0.5)),
-        grid=(steps,),
-        out_shape=(tokens,) * 4 + (jax.ShapeDtypeStruct((channels, share), jnp.float32),),
-        in_specs=[token_spec] * 4 + [plane_spec] * 2 + [filter_block],
-        out_specs=(token_spec,) * 4 + (filter_block,),
+        finish,
+        out_shape=tuple(pltpu.HBM(a.shape, a.dtype) for a in shapes),
+        in_specs=[in_vmem] * 5,
+        out_specs=(in_hbm,) * 5,
+        scratch_shapes=[pltpu.SemaphoreType.DMA((5,))],
         name="finish",
-    )(query_gate, key_gate, value_in, out_grad, conv, back, total)
+    )(*(pltpu.with_memory_space_constraint(a, pltpu.VMEM) for a in held))
 
 
 def solution(mesh):

time: 77 us -> 65.2 us (0.85)
  local copies, waits for them, and re-layouts: 10.2 us -> 0 us
  Pallas kernels: 65.4 us -> 64.5 us
    unnamed x22 -> x0, local copies, waits for them, and re-layouts: 10.2 us -> none
    pallas_call x2, Pallas kernels: 65.4 us -> 64.5 us  [the longest x1 63.1 us: shards(): pl.pallas_call(functools.partial(mixing, peers, (seq_len * parts) ** (-0....]
where the time goes in v1:
time: 65.2 us
  Pallas kernels  64.5 us (99%)
    pallas_call x1, Pallas kernels, shards(): pl.pallas_call(functools.partial(mixing, peers, (seq_len * parts) ** (-0....  63.1 us
    pallas_call x1, Pallas kernels, shards(): pl.pallas_call(finish, out_shape=tuple((pltpu.HBM(a.shape, a.dtype) for a...  1.39 us

profile of v1, /device:TPU:1, one launch (start us, length us, event | category | flops | bytes accessed | tf_op | source)
XLA Modules:
  0.0 65.2 jit_solution(7607950183365882528)
XLA Ops:
  0.6 63.1 %mixing.1 = (bf16[1,128,2048]{2,1,0:T(8,128)(2,1)S(1)}, bf16[1,128,2048]{2,1,0:T(8,128)(2,1)S(1)}, bf16[1,128,2048]{2,1,0:T(8,128)(2,1)S(1)}, bf16[1,128,2048]{2,1,0:T(8,128)(2,1)S(1)}, f32[64,512]{1,0:T(8,128)S(1)}) custom-call(bf16[128,2048]{1,0:T(8,128)(2,1)} %bitcast.4, bf16[128,2048]{1,0:T(8,128)(2,1)} %bitcast.5, bf16[128,2048]{1,0:T(8,128)(2,1)} %bitcast.6, ...), custom_call_target="tpu_custom_call" | custom-call | tf_op jit(solution)/shard_map/mixing/pallas_call | solution.py:492
  63.8 1.4 %finish.1 = (bf16[1,128,2048]{2,1,0:T(8,128)(2,1)}, bf16[1,128,2048]{2,1,0:T(8,128)(2,1)}, bf16[1,128,2048]{2,1,0:T(8,128)(2,1)}, bf16[1,128,2048]{2,1,0:T(8,128)(2,1)}, f32[64,512]{1,0:T(8,128)}) custom-call(bf16[1,128,2048]{2,1,0:T(8,128)(2,1)S(1)} %get-tuple-element.10.refs_0_, bf16[1,128,2048]{2,1,0:T(8,128)(2,1)S(1)} %get-tuple-element.11.refs_1_, ...), custom_call_target="tpu_custom_call" | custom-call | tf_op jit(solution)/shard_map/finish/pallas_call | solution.py:543

commit v2 on v1

--- a/solution.py
+++ b/solution.py
@@ -15,6 +15,7 @@
 BINS = 33
 GROUP = 16
 CHUNK = 11
+PIECES = 2
 ROOT = math.sqrt(0.5)
 
 
@@ -30,6 +31,7 @@
         jnp.asarray(forward, jnp.bfloat16),
         jnp.asarray(inverse, jnp.bfloat16),
         jnp.asarray(twist, jnp.float32),
+        jnp.asarray(np.eye(LANES), jnp.bfloat16),
     )
 
 
@@ -229,20 +231,21 @@
     forward_in,
     inverse_in,
     twist_in,
+    diagonal_in,
+    gate,
     mixed_out,
     query_grad,
-    key_grad,
-    value_grad,
+    back,
     filter_out,
-    gate,
+    conv,
     taps,
     forward,
     inverse,
     twist,
+    diagonal,
     sent,
     got,
     replied,
-    answer,
     packed,
     wide,
     filter_spec,
@@ -257,7 +260,6 @@
     recv_sem,
     term_sem,
     half_sem,
-    back_sem,
 ):
     me = lax.axis_index("ctx")
     dp = lax.axis_index("dp")
@@ -291,6 +293,7 @@
                 (forward_in, forward),
                 (inverse_in, inverse),
                 (twist_in, twist),
+                (diagonal_in, diagonal),
             ]
         )
     ]
@@ -301,22 +304,26 @@
         def body(t, carry):
             lanes = pl.ds(pl.multiple_of(t * LANES, LANES), LANES)
             product = gate[first, :, lanes].astype(jnp.float32) * gate[second, :, lanes].astype(jnp.float32)
-            flipped = jnp.transpose(product).astype(jnp.bfloat16)
+            flipped = lax.dot_general(
+                diagonal[...],
+                product.astype(jnp.bfloat16),
+                (((1,), (1,)), ((), ())),
+                preferred_element_type=jnp.float32,
+            ).astype(jnp.bfloat16)
             sent[slot, pl.ds(2 * t, 2)] = flipped.reshape(2, LANES // 2, LANES)
             return carry
 
         lax.fori_loop(0, peers // 2, body, 0)
         got[slot, me] = sent[slot, me]
 
-    def scatter(source, target, slot, sem_base):
+    def scatter(source, target, n):
         def body(i, carry):
             peer = lax.rem(me + i, peers)
-            last = sem_base + slot == 3
             pltpu.make_async_remote_copy(
-                src_ref=source.at[slot, peer],
-                dst_ref=target.at[slot, me],
-                send_sem=send_sem.at[sem_base + slot],
-                recv_sem=back_sem.at[me] if last else recv_sem.at[sem_base + slot],
+                src_ref=source.at[peer],
+                dst_ref=target.at[me],
+                send_sem=send_sem.at[n],
+                recv_sem=recv_sem.at[n],
                 device_id={"ctx": peer},
                 device_id_type=MESH,
             ).start()
@@ -324,27 +331,28 @@
 
         lax.fori_loop(1, peers, body, 0)
 
-    def whole(source, target, slot, sem_base):
+    def whole(source, target, n):
         part = pl.ds(0, peers - 1)
         return pltpu.make_async_remote_copy(
-            src_ref=source.at[slot, part],
-            dst_ref=target.at[slot, part],
-            send_sem=send_sem.at[sem_base + slot],
-            recv_sem=recv_sem.at[sem_base + slot],
+            src_ref=source.at[part],
+            dst_ref=target.at[part],
+            send_sem=send_sem.at[n],
+            recv_sem=recv_sem.at[n],
             device_id={"ctx": lax.rem(me + 1, peers)},
             device_id_type=MESH,
         )
 
     loads[0].wait()
     loads[1].wait()
+    loads[8].wait()
     gated(0, 1, 0)
     pl.semaphore_wait(barrier, peers - 1 + 4)
-    scatter(sent, got, 0, 0)
+    scatter(sent.at[0], got.at[0], 0)
     loads[2].wait()
     loads[3].wait()
     gated(2, 3, 1)
-    scatter(sent, got, 1, 0)
-    for load in loads[4:]:
+    scatter(sent.at[1], got.at[1], 1)
+    for load in loads[4:8]:
         load.wait()
 
     analyse(lambda j, rows: taps[rows, j * LANES : (j + 1) * LANES], twist, packed, channels)
@@ -354,8 +362,8 @@
 
     chunks(filter_step)
 
-    def convolve(slot, spectrum, product):
-        whole(sent, got, slot, 0).wait_recv()
+    def convolve(slot, spectrum, product, answer):
+        whole(sent.at[slot], got.at[slot], slot).wait_recv()
         analyse(lambda j, rows: got[slot, j, rows, :].astype(jnp.float32), twist, packed, channels)
 
         def step(k):
@@ -369,11 +377,11 @@
             replied[slot, j, rows, :] = values.astype(jnp.bfloat16)
 
         synthesise(wide, twist, write, channels)
-        answer[slot, me] = replied[slot, me]
-        scatter(replied, answer, slot, 2)
-
-    convolve(0, mixed_spec, times_plain)
-    convolve(1, grad_spec, times_conj)
+        answer[me] = replied[slot, me]
+        scatter(replied.at[slot], answer, slot + 2)
+
+    convolve(0, mixed_spec, times_plain, conv)
+    convolve(1, grad_spec, times_conj, back)
 
     def term_step(k):
         wide[k] = times(times_conj(mixed_spec[k], grad_spec[k]).astype(jnp.bfloat16), inverse[...])
@@ -400,8 +408,6 @@
         )
     for hop in hops:
         hop.start()
-    for hop in hops:
-        hop.wait_recv()
 
     def total(which):
         mine = term[pl.ds(line * 8 + which * 4, 4)].astype(jnp.float32)
@@ -409,6 +415,8 @@
             mine += term_got[i, pl.ds(which * 4, 4)].astype(jnp.float32)
         return mine
 
+    for hop in hops:
+        hop.wait_recv()
     half[...] = total(1 - side).astype(jnp.bfloat16)
     cross = pltpu.make_async_remote_copy(
         src_ref=half,
@@ -420,58 +428,61 @@
     )
     cross.start()
     kept = total(side)
+    for j in range(4):
+        filter_out[:, j * LANES : (j + 1) * LANES] = kept[j]
+
+    whole(replied.at[0], conv, 2).wait_recv()
+
+    def conv_tile(t, carry):
+        lanes = pl.ds(pl.multiple_of(t * LANES, LANES), LANES)
+        columns = turned_over(diagonal[...], conv[pl.ds(2 * t, 2)].reshape(LANES, LANES))
+        mixed_out[:, lanes] = (gate[2, :, lanes].astype(jnp.float32) * columns).astype(jnp.bfloat16)
+        query_grad[:, lanes] = (gate[3, :, lanes].astype(jnp.float32) * columns).astype(jnp.bfloat16)
+        return carry
+
+    lax.fori_loop(0, peers // 2, conv_tile, 0)
     cross.wait_recv()
-    kept += half_got[...].astype(jnp.float32)
     for j in range(4):
-        filter_out[:, j * LANES : (j + 1) * LANES] = kept[j] * scale
-
-    def tile(slot, t, first, second, first_out, second_out):
-        lanes = pl.ds(pl.multiple_of(t * LANES, LANES), LANES)
-        rows = answer[slot, pl.ds(2 * t, 2)].reshape(LANES, LANES)
-        wide_rows = jnp.transpose(rows.astype(jnp.float32))
-        first_out[0, :, lanes] = (gate[first, :, lanes].astype(jnp.float32) * wide_rows).astype(jnp.bfloat16)
-        second_out[0, :, lanes] = (gate[second, :, lanes].astype(jnp.float32) * wide_rows).astype(jnp.bfloat16)
-
-    whole(replied, answer, 0, 2).wait_recv()
-
-    def conv_tile(t, carry):
-        tile(0, t, 2, 3, mixed_out, query_grad)
-        return carry
-
-    lax.fori_loop(0, peers // 2, conv_tile, 0)
-
-    def back_tile(i, carry):
-        t = lax.rem(me // 2 + peers // 2 - i, peers // 2)
-        for source in (2 * t, 2 * t + 1):
-
-            @pl.when(source != me)
-            def _():
-                pltpu.make_async_remote_copy(
-                    src_ref=replied.at[1, source],
-                    dst_ref=answer.at[1, source],
-                    send_sem=send_sem.at[3],
-                    recv_sem=back_sem.at[source],
-                    device_id={"ctx": lax.rem(me + 1, peers)},
-                    device_id_type=MESH,
-                ).wait_recv()
-
-        tile(1, t, 1, 0, key_grad, value_grad)
-        return carry
-
-    lax.fori_loop(0, peers // 2, back_tile, 0)
+        lanes = slice(j * LANES, (j + 1) * LANES)
+        filter_out[:, lanes] = (filter_out[:, lanes] + half_got[j].astype(jnp.float32)) * scale
     for slot in range(2):
-        whole(sent, got, slot, 0).wait_send()
-        whole(replied, answer, slot, 2).wait_send()
+        whole(sent.at[slot], got.at[slot], slot).wait_send()
+    whole(replied.at[0], conv, 2).wait_send()
     for hop in hops:
         hop.wait_send()
     cross.wait_send()
-
-
-def finish(*refs):
-    held, out, sem = refs[:5], refs[5:10], refs[10]
-    copies = [pltpu.make_async_copy(a, b, sem.at[n]) for n, (a, b) in enumerate(zip(held, out))]
-    for copy in copies:
-        copy.start()
+    whole(replied.at[1], back, 3).wait()
+
+
+def turned_over(identity, rows):
+    return lax.dot_general(identity, rows, (((1,), (1,)), ((), ())), preferred_element_type=jnp.float32)
+
+
+def finish(steps, gate, mixed, query, back, total, mixed_out, query_grad, key_grad, value_grad, filter_grad, made, sem):
+    block, width = mixed.shape
+    rows = block // PIECES
+    copies = []
+
+    def send(source, target):
+        copies.append(pltpu.make_async_copy(source, target, sem.at[len(copies)]))
+        copies[-1].start()
+
+    for held, out in ((mixed, mixed_out), (query, query_grad)):
+        for n in range(PIECES):
+            part = pl.ds(n * rows, rows)
+            send(held.at[part], out.at[0, part])
+    send(total, filter_grad)
+    identity = lax.broadcasted_iota(jnp.int32, (block, block), 0) == lax.broadcasted_iota(
+        jnp.int32, (block, block), 1
+    )
+    identity = identity.astype(jnp.float32).astype(jnp.bfloat16)
+    owners = back.shape[0] // steps
+    for n in range(steps):
+        lanes = pl.ds(n * (width // steps), width // steps)
+        columns = turned_over(identity, back[n * owners : (n + 1) * owners].reshape(-1, block))
+        for slot, factor, out in ((0, 1, key_grad), (1, 0, value_grad)):
+            made[slot, :, lanes] = (columns * gate[factor, :, lanes].astype(jnp.float32)).astype(jnp.bfloat16)
+            send(made.at[slot, :, lanes], out.at[0, :, lanes])
     for copy in copies:
         copy.wait()
 
@@ -481,26 +492,32 @@
     channels, seq_len = filter_taps.shape
     peers = lax.axis_size("ctx")
     parts = lax.axis_size("dp")
-    forward, inverse, twist = tables()
+    forward, inverse, twist, diagonal = tables()
     in_hbm = pl.BlockSpec(memory_space=pltpu.HBM)
     in_vmem = pl.BlockSpec(memory_space=pltpu.VMEM)
     planes = (peers, channels, LANES)
     spectrum = pltpu.VMEM((BINS, channels, 2 * LANES), jnp.float32)
     share = seq_len // parts
     tokens = jax.ShapeDtypeStruct(query_gate.shape, jnp.bfloat16)
-    shapes = (tokens,) * 4 + (jax.ShapeDtypeStruct((channels, share), jnp.float32),)
+    filter_share = jax.ShapeDtypeStruct((channels, share), jnp.float32)
     held = pl.pallas_call(
         functools.partial(mixing, peers, (seq_len * parts) ** (-0.5)),
-        out_shape=tuple(pltpu.VMEM(a.shape, a.dtype) for a in shapes),
-        in_specs=[in_hbm] * 8,
+        out_shape=(
+            pltpu.VMEM((4, block, width), jnp.bfloat16),
+            pltpu.VMEM((block, width), jnp.bfloat16),
+            pltpu.VMEM((block, width), jnp.bfloat16),
+            pltpu.VMEM(planes, jnp.bfloat16),
+            pltpu.VMEM(filter_share.shape, filter_share.dtype),
+        ),
+        in_specs=[in_hbm] * 9,
         out_specs=(in_vmem,) * 5,
         scratch_shapes=[
-            pltpu.VMEM((4, block, width), jnp.bfloat16),
+            pltpu.VMEM(planes, jnp.bfloat16),
             pltpu.VMEM((channels, seq_len), jnp.float32),
             pltpu.VMEM((2 * LANES, 2 * LANES), jnp.bfloat16),
             pltpu.VMEM((2 * LANES, 2 * LANES), jnp.bfloat16),
             pltpu.VMEM((BINS, 2 * LANES), jnp.float32),
-            pltpu.VMEM((2,) + planes, jnp.bfloat16),
+            pltpu.VMEM((LANES, LANES), jnp.bfloat16),
             pltpu.VMEM((2,) + planes, jnp.bfloat16),
             pltpu.VMEM((2,) + planes, jnp.bfloat16),
             pltpu.VMEM((2,) + planes, jnp.bfloat16),
@@ -513,12 +530,11 @@
             pltpu.VMEM((3, 8, channels, LANES), jnp.bfloat16),
             pltpu.VMEM((4, channels, LANES), jnp.bfloat16),
             pltpu.VMEM((4, channels, LANES), jnp.bfloat16),
-            pltpu.SemaphoreType.DMA((8,)),
+            pltpu.SemaphoreType.DMA((9,)),
             pltpu.SemaphoreType.DMA((4,)),
             pltpu.SemaphoreType.DMA((4,)),
             pltpu.SemaphoreType.DMA((6,)),
             pltpu.SemaphoreType.DMA((2,)),
-            pltpu.SemaphoreType.DMA((peers,)),
         ],
         compiler_params=pltpu.CompilerParams(
             collective_id=0, has_side_effects=True, vmem_limit_bytes=32 << 20
@@ -536,16 +552,22 @@
                 forward,
                 inverse,
                 twist,
+                diagonal,
             )
         )
     )
 
+    steps = 4
     return pl.pallas_call(
-        finish,
-        out_shape=tuple(pltpu.HBM(a.shape, a.dtype) for a in shapes),
+        functools.partial(finish, steps),
+        out_shape=tuple(pltpu.HBM(a.shape, a.dtype) for a in (tokens,) * 4 + (filter_share,)),
         in_specs=[in_vmem] * 5,
         out_specs=(in_hbm,) * 5,
-        scratch_shapes=[pltpu.SemaphoreType.DMA((5,))],
+        scratch_shapes=[
+            pltpu.VMEM((2, block, width), jnp.bfloat16),
+            pltpu.SemaphoreType.DMA((2 * PIECES + 1 + 2 * steps,)),
+        ],
+        compiler_params=pltpu.CompilerParams(vmem_limit_bytes=16 << 20),
         name="finish",
     )(*(pltpu.with_memory_space_constraint(a, pltpu.VMEM) for a in held))
 

time: 65.2 us -> 61.8 us (0.948)
  Pallas kernels: 64.5 us -> 61 us
    pallas_call x1, Pallas kernels: 63.1 us -> 59.6 us  [shards(): pl.pallas_call(functools.partial(mixing, peers, (seq_len * parts) ** (-0....]
where the time goes in v2:
time: 61.8 us; the launch traced here: 61.7 us
  Pallas kernels  61 us (99%)
  between operations  0.64 us (1%)
    pallas_call x1, Pallas kernels, shards(): pl.pallas_call(functools.partial(mixing, peers, (seq_len * parts) ** (-0....  59.6 us
    pallas_call x1, Pallas kernels, shards(): pl.pallas_call(functools.partial(finish, steps), out_shape=tuple((pltpu.H...  1.46 us

profile of v2, /device:TPU:1, one launch (start us, length us, event | category | flops | bytes accessed | tf_op | source)
XLA Modules:
  0.0 61.7 jit_solution(11999951318742072171)
XLA Ops:
  0.6 59.6 %mixing.1 = (bf16[4,128,2048]{2,1,0:T(8,128)(2,1)S(1)}, bf16[128,2048]{1,0:T(8,128)(2,1)S(1)}, bf16[128,2048]{1,0:T(8,128)(2,1)S(1)}, bf16[32,64,128]{2,1,0:T(8,128)(2,1)S(1)}, f32[64,512]{1,0:T(8,128)S(1)}) custom-call(bf16[128,2048]{1,0:T(8,128)(2,1)} %bitcast.4, bf16[128,2048]{1,0:T(8,128)(2,1)} %bitcast.5, bf16[128,2048]{1,0:T(8,128)(2,1)} %bitcast.6, ...), custom_call_target="tpu_custom_call" | custom-call | tf_op jit(solution)/shard_map/mixing/pallas_call | solution.py:503
  60.2 1.5 %finish.1 = (bf16[1,128,2048]{2,1,0:T(8,128)(2,1)}, bf16[1,128,2048]{2,1,0:T(8,128)(2,1)}, bf16[1,128,2048]{2,1,0:T(8,128)(2,1)}, bf16[1,128,2048]{2,1,0:T(8,128)(2,1)}, f32[64,512]{1,0:T(8,128)}) custom-call(bf16[4,128,2048]{2,1,0:T(8,128)(2,1)S(1)} %get-tuple-element.10.gate, bf16[128,2048]{1,0:T(8,128)(2,1)S(1)} %get-tuple-element.11.mixed, ...), custom_call_target="tpu_custom_call" | custom-call | tf_op jit(solution)/shard_map/finish/pallas_call | solution.py:561

commit v3 on v2

--- a/solution.py
+++ b/solution.py
@@ -17,6 +17,11 @@
 CHUNK = 11
 PIECES = 2
 ROOT = math.sqrt(0.5)
+
+
+def in_two(matrix):
+    high = matrix.astype(jnp.bfloat16)
+    return jnp.asarray(np.stack([high, (matrix - high.astype(np.float64)).astype(jnp.bfloat16)]))
 
 
 def tables():
@@ -28,8 +33,8 @@
     turn = 2.0 * np.pi * (np.arange(BINS, dtype=np.float64)[:, None] * step[None, :]) / (64.0 * LANES)
     twist = np.concatenate([np.cos(turn), np.sin(turn)], axis=1)
     return (
-        jnp.asarray(forward, jnp.bfloat16),
-        jnp.asarray(inverse, jnp.bfloat16),
+        in_two(forward),
+        in_two(inverse),
         jnp.asarray(twist, jnp.float32),
         jnp.asarray(np.eye(LANES), jnp.bfloat16),
     )
@@ -169,8 +174,8 @@
                 else:
                     real = bins[k][0] * cos + bins[k][1] * sin
                     imag = bins[k][1] * cos - bins[k][0] * sin
-            packed[k, rows, :LANES] = real.astype(jnp.bfloat16)
-            packed[k, rows, LANES:] = imag.astype(jnp.bfloat16)
+            packed[k, rows, :LANES] = real
+            packed[k, rows, LANES:] = imag
         return carry
 
     lax.fori_loop(0, channels // GROUP, body, 0)
@@ -196,6 +201,15 @@
     lax.fori_loop(0, channels // GROUP, body, 0)
 
 
+def grouped(count, size, body):
+    def step(i, carry):
+        for n in range(size):
+            body(i * size + n, 0)
+        return carry
+
+    lax.fori_loop(0, count // size, step, 0)
+
+
 def chunks(body):
     def step(i, carry):
         body(pl.ds(i * CHUNK, CHUNK))
@@ -206,7 +220,11 @@
 
 def times(rows, matrix):
     flat = rows.reshape(-1, 2 * LANES)
-    out = jnp.dot(flat, matrix, preferred_element_type=jnp.float32)
+    high = flat.astype(jnp.bfloat16)
+    low = (flat - high.astype(jnp.float32)).astype(jnp.bfloat16)
+    out = jnp.dot(high, matrix[0], preferred_element_type=jnp.float32)
+    out += jnp.dot(high, matrix[1], preferred_element_type=jnp.float32)
+    out += jnp.dot(low, matrix[0], preferred_element_type=jnp.float32)
     return out.reshape(rows.shape)
 
 
@@ -268,19 +286,6 @@
 
     barrier = pltpu.get_barrier_semaphore()
 
-    def greet(i, carry):
-        pl.semaphore_signal(
-            barrier, inc=1, device_id={"ctx": lax.rem(me + i, peers)}, device_id_type=MESH
-        )
-        return carry
-
-    lax.fori_loop(1, peers, greet, 0)
-    for i in range(1, 4):
-        pl.semaphore_signal(
-            barrier, inc=1, device_id={"dp": lax.rem(line + i, 4) * 2 + side}, device_id_type=MESH
-        )
-    pl.semaphore_signal(barrier, inc=1, device_id={"dp": line * 2 + 1 - side}, device_id_type=MESH)
-
     loads = [
         pltpu.make_async_copy(source, target, load_sem.at[n])
         for n, (source, target) in enumerate(
@@ -297,8 +302,16 @@
             ]
         )
     ]
-    for load in loads:
+    for load in loads[:2] + loads[8:]:
         load.start()
+
+    for i in range(1, peers):
+        pl.semaphore_signal(barrier, inc=1, device_id={"ctx": lax.rem(me + i, peers)}, device_id_type=MESH)
+    for i in range(1, 4):
+        pl.semaphore_signal(
+            barrier, inc=1, device_id={"dp": lax.rem(line + i, 4) * 2 + side}, device_id_type=MESH
+        )
+    pl.semaphore_signal(barrier, inc=1, device_id={"dp": line * 2 + 1 - side}, device_id_type=MESH)
 
     def gated(first, second, slot):
         def body(t, carry):
@@ -313,7 +326,7 @@
             sent[slot, pl.ds(2 * t, 2)] = flipped.reshape(2, LANES // 2, LANES)
             return carry
 
-        lax.fori_loop(0, peers // 2, body, 0)
+        grouped(peers // 2, 4, body)
         got[slot, me] = sent[slot, me]
 
     def scatter(source, target, n):
@@ -345,6 +358,8 @@
     loads[0].wait()
     loads[1].wait()
     loads[8].wait()
+    for load in loads[2:8]:
+        load.start()
     gated(0, 1, 0)
     pl.semaphore_wait(barrier, peers - 1 + 4)
     scatter(sent.at[0], got.at[0], 0)
@@ -358,7 +373,7 @@
     analyse(lambda j, rows: taps[rows, j * LANES : (j + 1) * LANES], twist, packed, channels)
 
     def filter_step(k):
-        filter_spec[k] = times(packed[k], forward[...])
+        filter_spec[k] = times(packed[k], forward)
 
     chunks(filter_step)
 
@@ -367,9 +382,9 @@
         analyse(lambda j, rows: got[slot, j, rows, :].astype(jnp.float32), twist, packed, channels)
 
         def step(k):
-            spec = times(packed[k], forward[...])
+            spec = times(packed[k], forward)
             spectrum[k] = spec
-            wide[k] = times(product(filter_spec[k], spec).astype(jnp.bfloat16), inverse[...])
+            wide[k] = times(product(filter_spec[k], spec), inverse)
 
         chunks(step)
 
@@ -384,7 +399,7 @@
     convolve(1, grad_spec, times_conj, back)
 
     def term_step(k):
-        wide[k] = times(times_conj(mixed_spec[k], grad_spec[k]).astype(jnp.bfloat16), inverse[...])
+        wide[k] = times(times_conj(mixed_spec[k], grad_spec[k]), inverse)
 
     chunks(term_step)
 
@@ -514,14 +529,14 @@
         scratch_shapes=[
             pltpu.VMEM(planes, jnp.bfloat16),
             pltpu.VMEM((channels, seq_len), jnp.float32),
-            pltpu.VMEM((2 * LANES, 2 * LANES), jnp.bfloat16),
-            pltpu.VMEM((2 * LANES, 2 * LANES), jnp.bfloat16),
+            pltpu.VMEM((2, 2 * LANES, 2 * LANES), jnp.bfloat16),
+            pltpu.VMEM((2, 2 * LANES, 2 * LANES), jnp.bfloat16),
             pltpu.VMEM((BINS, 2 * LANES), jnp.float32),
             pltpu.VMEM((LANES, LANES), jnp.bfloat16),
             pltpu.VMEM((2,) + planes, jnp.bfloat16),
             pltpu.VMEM((2,) + planes, jnp.bfloat16),
             pltpu.VMEM((2,) + planes, jnp.bfloat16),
-            pltpu.VMEM((BINS, channels, 2 * LANES), jnp.bfloat16),
+            spectrum,
             spectrum,
             spectrum,
             spectrum,

time: 61.8 us -> 61.6 us (level)
  no operation moved by 1% of the time
where the time goes in v3:
time: 61.6 us; the launch traced here: 61.5 us
  Pallas kernels  60.8 us (99%)
  between operations  0.64 us (1%)
    pallas_call x1, Pallas kernels, shards(): pl.pallas_call(functools.partial(mixing, peers, (seq_len * parts) ** (-0....  59.4 us
    pallas_call x1, Pallas kernels, shards(): pl.pallas_call(functools.partial(finish, steps), out_shape=tuple((pltpu.H...  1.46 us

profile of v3, /device:TPU:1, one launch (start us, length us, event | category | flops | bytes accessed | tf_op | source)
XLA Modules:
  0.0 61.5 jit_solution(13277351432469760628)
XLA Ops:
  0.6 59.4 %mixing.1 = (bf16[4,128,2048]{2,1,0:T(8,128)(2,1)S(1)}, bf16[128,2048]{1,0:T(8,128)(2,1)S(1)}, bf16[128,2048]{1,0:T(8,128)(2,1)S(1)}, bf16[32,64,128]{2,1,0:T(8,128)(2,1)S(1)}, f32[64,512]{1,0:T(8,128)S(1)}) custom-call(bf16[128,2048]{1,0:T(8,128)(2,1)} %bitcast.4, bf16[128,2048]{1,0:T(8,128)(2,1)} %bitcast.5, bf16[128,2048]{1,0:T(8,128)(2,1)} %bitcast.6, ...), custom_call_target="tpu_custom_call" | custom-call | tf_op jit(solution)/shard_map/mixing/pallas_call | solution.py:518
  60.0 1.5 %finish.1 = (bf16[1,128,2048]{2,1,0:T(8,128)(2,1)}, bf16[1,128,2048]{2,1,0:T(8,128)(2,1)}, bf16[1,128,2048]{2,1,0:T(8,128)(2,1)}, bf16[1,128,2048]{2,1,0:T(8,128)(2,1)}, f32[64,512]{1,0:T(8,128)}) custom-call(bf16[4,128,2048]{2,1,0:T(8,128)(2,1)S(1)} %get-tuple-element.10.gate, bf16[128,2048]{1,0:T(8,128)(2,1)S(1)} %get-tuple-element.11.mixed, ...), custom_call_target="tpu_custom_call" | custom-call | tf_op jit(solution)/shard_map/finish/pallas_call | solution.py:576

commit v4 on v3

--- a/solution.py
+++ b/solution.py
@@ -15,7 +15,7 @@
 BINS = 33
 GROUP = 16
 CHUNK = 11
-PIECES = 2
+PIECES = 1
 ROOT = math.sqrt(0.5)
 
 
@@ -342,7 +342,8 @@
             ).start()
             return carry
 
-        lax.fori_loop(1, peers, body, 0)
+        for i in range(1, peers):
+            body(i, 0)
 
     def whole(source, target, n):
         part = pl.ds(0, peers - 1)
@@ -455,7 +456,7 @@
         query_grad[:, lanes] = (gate[3, :, lanes].astype(jnp.float32) * columns).astype(jnp.bfloat16)
         return carry
 
-    lax.fori_loop(0, peers // 2, conv_tile, 0)
+    grouped(peers // 2, 4, conv_tile)
     cross.wait_recv()
     for j in range(4):
         lanes = slice(j * LANES, (j + 1) * LANES)
@@ -572,7 +573,7 @@
         )
     )
 
-    steps = 4
+    steps = 2
     return pl.pallas_call(
         functools.partial(finish, steps),
         out_shape=tuple(pltpu.HBM(a.shape, a.dtype) for a in (tokens,) * 4 + (filter_share,)),

time: 61.6 us -> 61.5 us (level)
  no operation moved by 1% of the time
where the time goes in v4:
time: 61.5 us; the launch traced here: 61.4 us
  Pallas kernels  60.8 us (99%)
  between operations  0.64 us (1%)
    pallas_call x1, Pallas kernels, shards(): pl.pallas_call(functools.partial(mixing, peers, (seq_len * parts) ** (-0....  59.4 us
    pallas_call x1, Pallas kernels, shards(): pl.pallas_call(functools.partial(finish, steps), out_shape=tuple((pltpu.H...  1.41 us

profile of v4, /device:TPU:1, one launch (start us, length us, event | category | flops | bytes accessed | tf_op | source)
XLA Modules:
  0.0 61.4 jit_solution(11816840397234818017)
XLA Ops:
  0.6 59.4 %mixing.1 = (bf16[4,128,2048]{2,1,0:T(8,128)(2,1)S(1)}, bf16[128,2048]{1,0:T(8,128)(2,1)S(1)}, bf16[128,2048]{1,0:T(8,128)(2,1)S(1)}, bf16[32,64,128]{2,1,0:T(8,128)(2,1)S(1)}, f32[64,512]{1,0:T(8,128)S(1)}) custom-call(bf16[128,2048]{1,0:T(8,128)(2,1)} %bitcast.4, bf16[128,2048]{1,0:T(8,128)(2,1)} %bitcast.5, bf16[128,2048]{1,0:T(8,128)(2,1)} %bitcast.6, ...), custom_call_target="tpu_custom_call" | custom-call | tf_op jit(solution)/shard_map/mixing/pallas_call | solution.py:519
  60.0 1.4 %finish.1 = (bf16[1,128,2048]{2,1,0:T(8,128)(2,1)}, bf16[1,128,2048]{2,1,0:T(8,128)(2,1)}, bf16[1,128,2048]{2,1,0:T(8,128)(2,1)}, bf16[1,128,2048]{2,1,0:T(8,128)(2,1)}, f32[64,512]{1,0:T(8,128)}) custom-call(bf16[4,128,2048]{2,1,0:T(8,128)(2,1)S(1)} %get-tuple-element.10.gate, bf16[128,2048]{1,0:T(8,128)(2,1)S(1)} %get-tuple-element.11.mixed, ...), custom_call_target="tpu_custom_call" | custom-call | tf_op jit(solution)/shard_map/finish/pallas_call | solution.py:577
